TPU v7x, 512 devices: a whole 4x4x16 slice. The times are simulated.
512 devices in a mesh: grp: 16 (over x, z_hi, core), hid: 32 (over y, z_lo).
Axes of the slice: x: 4, y: 4, z: 16 (z_hi: 2, z_lo: 8; z = z_hi * 8 + z_lo), core: 2. Of those that a mesh axis runs over, the one named last changes fastest.
Arguments:
- acts: bfloat16 [2, 512, 64, 4096], P(None, 'grp', None, 'hid'), may hold values from -6 to 6
- cotangents: bfloat16 [2, 512, 64, 4096], P(None, 'grp', None, 'hid'), may hold values from -6 to 6
- adapter_down_weight: bfloat16 [2, 16, 4096], P(None, None, 'hid'), may hold values from -0.09375 to 0.09375
- adapter_up_weight: bfloat16 [2, 4096, 16], P(None, 'hid'), may hold values from -0.09375 to 0.09375
- lengths: int32 [512], P('grp'), may hold values from 17 to 64
Outputs:
- similarity: float32 [512, 512], P('hid', 'grp')
All inputs are finite; a program needn't handle non-finite values.
Results may differ from a plain program's by a relative error of at most 0.00089.
Values may be sent and summed in bfloat16 or wider, within the bound.
No kernel may reach another device: no remote copies, remote signals or barrier semaphores. Data moves between devices by JAX's collectives and lax.ppermute only.
A program may use at most 64 MiB of HBM per device.

v0:
```python
import jax
import jax.numpy as jnp
from jax import lax
from jax.sharding import PartitionSpec as P


def passed_along(block, axis, distance):
    devices = range(lax.axis_size(axis))
    route = [((i - distance) % len(devices), i) for i in devices]
    return lax.ppermute(block, axis, route)


def local(acts, cotangents, adapter_down_weight, adapter_up_weight, lengths):
    layers, count, positions, width = acts.shape
    mask = (lax.broadcasted_iota(jnp.int32, (count, positions), 1) < lengths[:, None]).astype(
        jnp.bfloat16
    )
    masked_values = cotangents * mask[None, :, :, None]
    up_factor = jnp.einsum(
        "mcoj,mju->mcou", masked_values, adapter_up_weight, preferred_element_type=jnp.float32
    )
    down_factor = jnp.einsum(
        "bwmv,bhv->bwmh", acts, adapter_down_weight, preferred_element_type=jnp.float32
    )
    up_sum, down_sum = lax.psum((up_factor, down_factor), "hid")
    grad_down = jnp.einsum(
        "lesr,lesd->elrd", up_sum.astype(jnp.bfloat16), acts, preferred_element_type=jnp.float32
    )
    grad_up = jnp.einsum(
        "lesd,lesr->elrd",
        masked_values,
        down_sum.astype(jnp.bfloat16),
        preferred_element_type=jnp.float32,
    )
    flat = jnp.concatenate([grad_down, grad_up], axis=2).astype(jnp.bfloat16).reshape(count, -1)
    wide = flat.astype(jnp.float32)
    partial_sq = jnp.sum(wide * wide, axis=1)
    groups = lax.axis_size("grp")
    group_index = lax.axis_index("grp")
    total = count * groups

    def tile_of(visitor):
        return lax.dot_general(
            visitor, flat, (((1,), (1,)), ((), ())), preferred_element_type=jnp.float32
        )

    def turn(step, carry):
        accum, visitor = carry
        owner = (group_index - step) % groups
        accum = lax.dynamic_update_slice(accum, tile_of(visitor), (owner * count, jnp.int32(0)))
        visitor = passed_along(visitor, "grp", 1)
        return (accum, visitor)

    start_acc = jnp.zeros((total, count), jnp.float32)
    accum, visitor = lax.fori_loop(0, groups - 1, turn, (start_acc, flat))
    owner = (group_index - (groups - 1)) % groups
    accum = lax.dynamic_update_slice(accum, tile_of(visitor), (owner * count, jnp.int32(0)))
    shards = lax.axis_size("hid")
    rows_here = total // shards
    share = lax.psum_scatter(accum, "hid", scatter_dimension=0, tiled=True)
    own = lax.psum(partial_sq, "hid")
    every = lax.all_gather(own, "grp", axis=0, tiled=True)
    column_sq = lax.dynamic_slice_in_dim(every, lax.axis_index("hid") * rows_here, rows_here, 0)
    return share * lax.rsqrt(column_sq + 1e-06)[:, None] * lax.rsqrt(own + 1e-06)[None, :]


def solution(mesh):
    return jax.shard_map(
        local,
        mesh=mesh,
        in_specs=(
            P(None, "grp", None, "hid"),
            P(None, "grp", None, "hid"),
            P(None, None, "hid"),
            P(None, "hid", None),
            P("grp"),
        ),
        out_specs=P("hid", "grp"),
        check_vma=False,
    )
```

profile of v0, /device:TPU:6, one launch (start us, length us, event | category | flops | bytes accessed | tf_op | source)
XLA Modules:
  0.0 917.0 jit_solution(9859896968988160178)
XLA Ops:
  7.2 2.1 fusion.4
  11.3 256.2 %all-reduce.3 = (bf16[2,32,64,16]{2,3,0,1:T(8,128)(2,1)S(1)}, bf16[2,32,64,16]{2,3,0,1:T(8,128)(2,1)S(1)}) all-reduce(f32[2,32,64,16]{2,3,0,1:T(8,128)S(1)} %fusion.4, f32[2,32,64,16]{2,3,0,1:T(8,128)S(1)} %fusion), channel_id=1, replica_groups=mesh['grp'=16,'hid'=32] {'hid'}, use_global_device_ids=true, to_apply=%region_1.0 | all-reduce | flops 131072 | bytes 786432 | tf_op jit(solution)/shard_map/psum | solution.py:25
  269.9 404.2 %while.17 = (s32[]{:T(128)}, f32[512,32]{1,0:T(8,128)S(1)}, bf16[32,8192]{1,0:T(8,128)(2,1)S(1)}, bf16[32,8192]{1,0:T(8,128)(2,1)S(1)}, s32[]{:T(128)}, /*index=...) while((s32[]{:T(128)}, f32[512,32]{1,0:T(8,128)S(1)}, ...), condition=%wide.region_3.4_spmd, body=%wide.region_2.0_spmd.sunk | while | flops 16777232 | bytes 4211008 | solution.py:55
  269.9 1.9 collective-permute-start
  272.1 32.2 %collective-permute-done = bf16[32,8192]{1,0:T(8,128)(2,1)S(1)} collective-permute-done((bf16[32,8192]{1,0:T(8,128)(2,1)S(1)}, bf16[32,8192]{1,0:T(8,128)(2,1)S(1)}, u32[]{:S(2)}, u32[]{:S(2)}) %collective-permute-start) | collective-permute-done | bytes 524320 | tf_op jit(solution)/shard_map/while/body/eval_jaxpr/ppermute | solution.py:10
  304.4 1.9 collective-permute-start
  306.6 21.9 %collective-permute-done = bf16[32,8192]{1,0:T(8,128)(2,1)S(1)} collective-permute-done((bf16[32,8192]{1,0:T(8,128)(2,1)S(1)}, bf16[32,8192]{1,0:T(8,128)(2,1)S(1)}, u32[]{:S(2)}, u32[]{:S(2)}) %collective-permute-start) | collective-permute-done | bytes 524320 | tf_op jit(solution)/shard_map/while/body/eval_jaxpr/ppermute | solution.py:10
  328.6 1.9 collective-permute-start
  330.8 21.5 %collective-permute-done = bf16[32,8192]{1,0:T(8,128)(2,1)S(1)} collective-permute-done((bf16[32,8192]{1,0:T(8,128)(2,1)S(1)}, bf16[32,8192]{1,0:T(8,128)(2,1)S(1)}, u32[]{:S(2)}, u32[]{:S(2)}) %collective-permute-start) | collective-permute-done | bytes 524320 | tf_op jit(solution)/shard_map/while/body/eval_jaxpr/ppermute | solution.py:10
  352.4 1.9 collective-permute-start
  354.6 24.9 %collective-permute-done = bf16[32,8192]{1,0:T(8,128)(2,1)S(1)} collective-permute-done((bf16[32,8192]{1,0:T(8,128)(2,1)S(1)}, bf16[32,8192]{1,0:T(8,128)(2,1)S(1)}, u32[]{:S(2)}, u32[]{:S(2)}) %collective-permute-start) | collective-permute-done | bytes 524320 | tf_op jit(solution)/shard_map/while/body/eval_jaxpr/ppermute | solution.py:10
  379.6 1.9 collective-permute-start
  381.8 25.2 %collective-permute-done = bf16[32,8192]{1,0:T(8,128)(2,1)S(1)} collective-permute-done((bf16[32,8192]{1,0:T(8,128)(2,1)S(1)}, bf16[32,8192]{1,0:T(8,128)(2,1)S(1)}, u32[]{:S(2)}, u32[]{:S(2)}) %collective-permute-start) | collective-permute-done | bytes 524320 | tf_op jit(solution)/shard_map/while/body/eval_jaxpr/ppermute | solution.py:10
  407.0 1.9 collective-permute-start
  409.2 24.9 %collective-permute-done = bf16[32,8192]{1,0:T(8,128)(2,1)S(1)} collective-permute-done((bf16[32,8192]{1,0:T(8,128)(2,1)S(1)}, bf16[32,8192]{1,0:T(8,128)(2,1)S(1)}, u32[]{:S(2)}, u32[]{:S(2)}) %collective-permute-start) | collective-permute-done | bytes 524320 | tf_op jit(solution)/shard_map/while/body/eval_jaxpr/ppermute | solution.py:10
  434.1 1.9 collective-permute-start
  436.3 25.2 %collective-permute-done = bf16[32,8192]{1,0:T(8,128)(2,1)S(1)} collective-permute-done((bf16[32,8192]{1,0:T(8,128)(2,1)S(1)}, bf16[32,8192]{1,0:T(8,128)(2,1)S(1)}, u32[]{:S(2)}, u32[]{:S(2)}) %collective-permute-start) | collective-permute-done | bytes 524320 | tf_op jit(solution)/shard_map/while/body/eval_jaxpr/ppermute | solution.py:10
  461.5 1.9 collective-permute-start
  463.8 24.9 %collective-permute-done = bf16[32,8192]{1,0:T(8,128)(2,1)S(1)} collective-permute-done((bf16[32,8192]{1,0:T(8,128)(2,1)S(1)}, bf16[32,8192]{1,0:T(8,128)(2,1)S(1)}, u32[]{:S(2)}, u32[]{:S(2)}) %collective-permute-start) | collective-permute-done | bytes 524320 | tf_op jit(solution)/shard_map/while/body/eval_jaxpr/ppermute | solution.py:10
  490.9 25.2 %collective-permute-done = bf16[32,8192]{1,0:T(8,128)(2,1)S(1)} collective-permute-done((bf16[32,8192]{1,0:T(8,128)(2,1)S(1)}, bf16[32,8192]{1,0:T(8,128)(2,1)S(1)}, u32[]{:S(2)}, u32[]{:S(2)}) %collective-permute-start) | collective-permute-done | bytes 524320 | tf_op jit(solution)/shard_map/while/body/eval_jaxpr/ppermute | solution.py:10
  518.3 24.9 %collective-permute-done = bf16[32,8192]{1,0:T(8,128)(2,1)S(1)} collective-permute-done((bf16[32,8192]{1,0:T(8,128)(2,1)S(1)}, bf16[32,8192]{1,0:T(8,128)(2,1)S(1)}, u32[]{:S(2)}, u32[]{:S(2)}) %collective-permute-start) | collective-permute-done | bytes 524320 | tf_op jit(solution)/shard_map/while/body/eval_jaxpr/ppermute | solution.py:10
  543.2 1.9 collective-permute-start
  545.5 25.2 %collective-permute-done = bf16[32,8192]{1,0:T(8,128)(2,1)S(1)} collective-permute-done((bf16[32,8192]{1,0:T(8,128)(2,1)S(1)}, bf16[32,8192]{1,0:T(8,128)(2,1)S(1)}, u32[]{:S(2)}, u32[]{:S(2)}) %collective-permute-start) | collective-permute-done | bytes 524320 | tf_op jit(solution)/shard_map/while/body/eval_jaxpr/ppermute | solution.py:10
  570.7 1.9 collective-permute-start
  572.9 24.9 %collective-permute-done = bf16[32,8192]{1,0:T(8,128)(2,1)S(1)} collective-permute-done((bf16[32,8192]{1,0:T(8,128)(2,1)S(1)}, bf16[32,8192]{1,0:T(8,128)(2,1)S(1)}, u32[]{:S(2)}, u32[]{:S(2)}) %collective-permute-start) | collective-permute-done | bytes 524320 | tf_op jit(solution)/shard_map/while/body/eval_jaxpr/ppermute | solution.py:10
  600.0 25.2 %collective-permute-done = bf16[32,8192]{1,0:T(8,128)(2,1)S(1)} collective-permute-done((bf16[32,8192]{1,0:T(8,128)(2,1)S(1)}, bf16[32,8192]{1,0:T(8,128)(2,1)S(1)}, u32[]{:S(2)}, u32[]{:S(2)}) %collective-permute-start) | collective-permute-done | bytes 524320 | tf_op jit(solution)/shard_map/while/body/eval_jaxpr/ppermute | solution.py:10
  627.4 24.9 %collective-permute-done = bf16[32,8192]{1,0:T(8,128)(2,1)S(1)} collective-permute-done((bf16[32,8192]{1,0:T(8,128)(2,1)S(1)}, bf16[32,8192]{1,0:T(8,128)(2,1)S(1)}, u32[]{:S(2)}, u32[]{:S(2)}) %collective-permute-start) | collective-permute-done | bytes 524320 | tf_op jit(solution)/shard_map/while/body/eval_jaxpr/ppermute | solution.py:10
  652.3 1.9 collective-permute-start
  654.6 19.5 %collective-permute-done = bf16[32,8192]{1,0:T(8,128)(2,1)S(1)} collective-permute-done((bf16[32,8192]{1,0:T(8,128)(2,1)S(1)}, bf16[32,8192]{1,0:T(8,128)(2,1)S(1)}, u32[]{:S(2)}, u32[]{:S(2)}) %collective-permute-start) | collective-permute-done | bytes 524320 | tf_op jit(solution)/shard_map/while/body/eval_jaxpr/ppermute | solution.py:10
  675.3 115.3 %psum.23 = f32[32]{0:T(128)S(1)} all-reduce(f32[32]{0:T(128)S(1)} %get-tuple-element.153), channel_id=1, replica_groups=mesh['grp'=16,'hid'=32] {'hid'}, use_global_device_ids=true, to_apply=%region_6.7 | all-reduce | flops 32 | bytes 256 | tf_op jit(solution)/shard_map/psum | solution.py:61
  792.8 57.2 %all-reduce = f32[512]{0:T(512)S(1)} all-reduce(f32[512]{0:T(512)S(1)} %dynamic-update-slice), channel_id=1, replica_groups=mesh['grp'=16,'hid'=32] {'grp'}, use_global_device_ids=true, to_apply=%add | all-reduce | flops 512 | bytes 4096
  850.1 58.7 %reduce-scatter.2.cloned.1.call-done = f32[16,32]{1,0:T(8,128)} async-done(((f32[512,32]{1,0:T(8,128)}), f32[16,32]{1,0:T(8,128)}) %reduce-scatter.2.cloned.1.call-update) | async-done | bytes 2064 | tf_op jit(solution)/shard_map/reduce_scatter | solution.py:60
  (63 shorter events, 21.3 us)
Async XLA Ops:
  6.5 0.7 copy-start
  6.5 2.9 copy-start.4
  6.5 902.2 %reduce-scatter.2.cloned.1.call-start = ((), (), s32[]{:S(2)}) async-start(), calls=%async_computation.1 | async-start | bytes 270336 | tf_op jit(solution)/shard_map/reduce_scatter | solution.py:60
  7.2 2.1 copy-start.3
  9.4 0.7 copy-start.5
  267.5 1.2 copy-start.1
  269.9 34.5 %collective-permute-start = (bf16[32,8192]{1,0:T(8,128)(2,1)S(1)}, bf16[32,8192]{1,0:T(8,128)(2,1)S(1)}, u32[]{:S(2)}, u32[]{:S(2)}) collective-permute-start(bf16[32,8192]{1,0:T(8,128)(2,1)S(1)} %copy.34), channel_id=1, source_target_pairs={{480,0},{0,32},{32,64},{64,96},{96,128},{128,160},{160,192},{192,2... | collective-permute-start | bytes 1572872 | tf_op jit(solution)/shard_map/while/body/eval_jaxpr/ppermute | solution.py:10
  304.4 24.1 %collective-permute-start = (bf16[32,8192]{1,0:T(8,128)(2,1)S(1)}, bf16[32,8192]{1,0:T(8,128)(2,1)S(1)}, u32[]{:S(2)}, u32[]{:S(2)}) collective-permute-start(bf16[32,8192]{1,0:T(8,128)(2,1)S(1)} %copy.34), channel_id=1, source_target_pairs={{480,0},{0,32},{32,64},{64,96},{96,128},{128,160},{160,192},{192,2... | collective-permute-start | bytes 1572872 | tf_op jit(solution)/shard_map/while/body/eval_jaxpr/ppermute | solution.py:10
  328.6 23.8 %collective-permute-start = (bf16[32,8192]{1,0:T(8,128)(2,1)S(1)}, bf16[32,8192]{1,0:T(8,128)(2,1)S(1)}, u32[]{:S(2)}, u32[]{:S(2)}) collective-permute-start(bf16[32,8192]{1,0:T(8,128)(2,1)S(1)} %copy.34), channel_id=1, source_target_pairs={{480,0},{0,32},{32,64},{64,96},{96,128},{128,160},{160,192},{192,2... | collective-permute-start | bytes 1572872 | tf_op jit(solution)/shard_map/while/body/eval_jaxpr/ppermute | solution.py:10
  352.4 27.1 %collective-permute-start = (bf16[32,8192]{1,0:T(8,128)(2,1)S(1)}, bf16[32,8192]{1,0:T(8,128)(2,1)S(1)}, u32[]{:S(2)}, u32[]{:S(2)}) collective-permute-start(bf16[32,8192]{1,0:T(8,128)(2,1)S(1)} %copy.34), channel_id=1, source_target_pairs={{480,0},{0,32},{32,64},{64,96},{96,128},{128,160},{160,192},{192,2... | collective-permute-start | bytes 1572872 | tf_op jit(solution)/shard_map/while/body/eval_jaxpr/ppermute | solution.py:10
  379.6 27.4 %collective-permute-start = (bf16[32,8192]{1,0:T(8,128)(2,1)S(1)}, bf16[32,8192]{1,0:T(8,128)(2,1)S(1)}, u32[]{:S(2)}, u32[]{:S(2)}) collective-permute-start(bf16[32,8192]{1,0:T(8,128)(2,1)S(1)} %copy.34), channel_id=1, source_target_pairs={{480,0},{0,32},{32,64},{64,96},{96,128},{128,160},{160,192},{192,2... | collective-permute-start | bytes 1572872 | tf_op jit(solution)/shard_map/while/body/eval_jaxpr/ppermute | solution.py:10
  407.0 27.1 %collective-permute-start = (bf16[32,8192]{1,0:T(8,128)(2,1)S(1)}, bf16[32,8192]{1,0:T(8,128)(2,1)S(1)}, u32[]{:S(2)}, u32[]{:S(2)}) collective-permute-start(bf16[32,8192]{1,0:T(8,128)(2,1)S(1)} %copy.34), channel_id=1, source_target_pairs={{480,0},{0,32},{32,64},{64,96},{96,128},{128,160},{160,192},{192,2... | collective-permute-start | bytes 1572872 | tf_op jit(solution)/shard_map/while/body/eval_jaxpr/ppermute | solution.py:10
  434.1 27.4 %collective-permute-start = (bf16[32,8192]{1,0:T(8,128)(2,1)S(1)}, bf16[32,8192]{1,0:T(8,128)(2,1)S(1)}, u32[]{:S(2)}, u32[]{:S(2)}) collective-permute-start(bf16[32,8192]{1,0:T(8,128)(2,1)S(1)} %copy.34), channel_id=1, source_target_pairs={{480,0},{0,32},{32,64},{64,96},{96,128},{128,160},{160,192},{192,2... | collective-permute-start | bytes 1572872 | tf_op jit(solution)/shard_map/while/body/eval_jaxpr/ppermute | solution.py:10
  461.5 27.1 %collective-permute-start = (bf16[32,8192]{1,0:T(8,128)(2,1)S(1)}, bf16[32,8192]{1,0:T(8,128)(2,1)S(1)}, u32[]{:S(2)}, u32[]{:S(2)}) collective-permute-start(bf16[32,8192]{1,0:T(8,128)(2,1)S(1)} %copy.34), channel_id=1, source_target_pairs={{480,0},{0,32},{32,64},{64,96},{96,128},{128,160},{160,192},{192,2... | collective-permute-start | bytes 1572872 | tf_op jit(solution)/shard_map/while/body/eval_jaxpr/ppermute | solution.py:10
  488.7 27.4 %collective-permute-start = (bf16[32,8192]{1,0:T(8,128)(2,1)S(1)}, bf16[32,8192]{1,0:T(8,128)(2,1)S(1)}, u32[]{:S(2)}, u32[]{:S(2)}) collective-permute-start(bf16[32,8192]{1,0:T(8,128)(2,1)S(1)} %copy.34), channel_id=1, source_target_pairs={{480,0},{0,32},{32,64},{64,96},{96,128},{128,160},{160,192},{192,2... | collective-permute-start | bytes 1572872 | tf_op jit(solution)/shard_map/while/body/eval_jaxpr/ppermute | solution.py:10
  516.1 27.1 %collective-permute-start = (bf16[32,8192]{1,0:T(8,128)(2,1)S(1)}, bf16[32,8192]{1,0:T(8,128)(2,1)S(1)}, u32[]{:S(2)}, u32[]{:S(2)}) collective-permute-start(bf16[32,8192]{1,0:T(8,128)(2,1)S(1)} %copy.34), channel_id=1, source_target_pairs={{480,0},{0,32},{32,64},{64,96},{96,128},{128,160},{160,192},{192,2... | collective-permute-start | bytes 1572872 | tf_op jit(solution)/shard_map/while/body/eval_jaxpr/ppermute | solution.py:10
  543.2 27.4 %collective-permute-start = (bf16[32,8192]{1,0:T(8,128)(2,1)S(1)}, bf16[32,8192]{1,0:T(8,128)(2,1)S(1)}, u32[]{:S(2)}, u32[]{:S(2)}) collective-permute-start(bf16[32,8192]{1,0:T(8,128)(2,1)S(1)} %copy.34), channel_id=1, source_target_pairs={{480,0},{0,32},{32,64},{64,96},{96,128},{128,160},{160,192},{192,2... | collective-permute-start | bytes 1572872 | tf_op jit(solution)/shard_map/while/body/eval_jaxpr/ppermute | solution.py:10
  570.7 27.1 %collective-permute-start = (bf16[32,8192]{1,0:T(8,128)(2,1)S(1)}, bf16[32,8192]{1,0:T(8,128)(2,1)S(1)}, u32[]{:S(2)}, u32[]{:S(2)}) collective-permute-start(bf16[32,8192]{1,0:T(8,128)(2,1)S(1)} %copy.34), channel_id=1, source_target_pairs={{480,0},{0,32},{32,64},{64,96},{96,128},{128,160},{160,192},{192,2... | collective-permute-start | bytes 1572872 | tf_op jit(solution)/shard_map/while/body/eval_jaxpr/ppermute | solution.py:10
  597.8 27.4 %collective-permute-start = (bf16[32,8192]{1,0:T(8,128)(2,1)S(1)}, bf16[32,8192]{1,0:T(8,128)(2,1)S(1)}, u32[]{:S(2)}, u32[]{:S(2)}) collective-permute-start(bf16[32,8192]{1,0:T(8,128)(2,1)S(1)} %copy.34), channel_id=1, source_target_pairs={{480,0},{0,32},{32,64},{64,96},{96,128},{128,160},{160,192},{192,2... | collective-permute-start | bytes 1572872 | tf_op jit(solution)/shard_map/while/body/eval_jaxpr/ppermute | solution.py:10
  625.2 27.1 %collective-permute-start = (bf16[32,8192]{1,0:T(8,128)(2,1)S(1)}, bf16[32,8192]{1,0:T(8,128)(2,1)S(1)}, u32[]{:S(2)}, u32[]{:S(2)}) collective-permute-start(bf16[32,8192]{1,0:T(8,128)(2,1)S(1)} %copy.34), channel_id=1, source_target_pairs={{480,0},{0,32},{32,64},{64,96},{96,128},{128,160},{160,192},{192,2... | collective-permute-start | bytes 1572872 | tf_op jit(solution)/shard_map/while/body/eval_jaxpr/ppermute | solution.py:10
  652.3 21.7 %collective-permute-start = (bf16[32,8192]{1,0:T(8,128)(2,1)S(1)}, bf16[32,8192]{1,0:T(8,128)(2,1)S(1)}, u32[]{:S(2)}, u32[]{:S(2)}) collective-permute-start(bf16[32,8192]{1,0:T(8,128)(2,1)S(1)} %copy.34), channel_id=1, source_target_pairs={{480,0},{0,32},{32,64},{64,96},{96,128},{128,160},{160,192},{192,2... | collective-permute-start | bytes 1572872 | tf_op jit(solution)/shard_map/while/body/eval_jaxpr/ppermute | solution.py:10
  674.5 0.7 copy-start.2
Sparse Core Ops, SparseCore 0:
  675.4 233.2 reduce-scatter.1
where the time goes:
time: 918 us; the launch traced here: 917 us
  blocking collectives  429 us (47%)
  waiting for transfers between devices  429 us (47%)
  starting transfers between devices  28.8 us (3%)
  between operations  14.1 us (2%)
    ppermute x15, waiting for transfers between devices, passed_along(): return lax.ppermute(block, axis, route)  370 us
    psum x1, blocking collectives, local(): up_sum, down_sum = lax.psum((up_factor, down_factor), 'hid')  256 us
    psum x1, blocking collectives, local(): own = lax.psum(partial_sq, 'hid')  115 us
    reduce_scatter x1, waiting for transfers between devices, local(): share = lax.psum_scatter(accum, 'hid', scatter_dimension=0, tiled=True)  58.7 us
    unnamed x1, blocking collectives  57.2 us
    ppermute x15, starting transfers between devices, passed_along(): return lax.ppermute(block, axis, route)  28.8 us
  transfers between devices with their start and end apart: 16, of which 16 were waited for; matrix products, arithmetic and copies ran while one was open for 1% of the time, Pallas kernels for 0%

commit v1 on v0

v1 whole, which is shorter than its diff:
```python
import jax
import jax.numpy as jnp
from jax import lax
from jax.sharding import Mesh, PartitionSpec as P

F32 = jnp.float32
BF16 = jnp.bfloat16


def swap(block, axes):
    return lax.all_to_all(block, axes, 0, 0, tiled=True)


def local(acts, cotangents, adapter_down_weight, adapter_up_weight, lengths):
    layers, count, positions, width = acts.shape
    rank = adapter_down_weight.shape[1]
    up = jnp.einsum("lesd,ldr->lres", cotangents, adapter_up_weight, preferred_element_type=F32)
    down = jnp.einsum("lesd,lrd->lres", acts, adapter_down_weight, preferred_element_type=F32)
    live = lax.broadcasted_iota(jnp.int32, (count, positions), 1) < lengths[:, None]
    partial = jnp.where(live, jnp.stack([up, down]), 0.0)
    rows = 2 * layers * rank
    partial = partial.reshape(rows, 4, count * positions // 4).transpose(1, 0, 2)
    partial = jnp.sum(swap(partial, "y"), 0)
    partial = partial.reshape(8, rows // 8, -1)
    mine = jnp.sum(swap(partial, "zl"), 0).astype(BF16)
    whole = swap(jnp.broadcast_to(mine, (8,) + mine.shape), "zl").reshape(rows, -1)
    whole = swap(jnp.broadcast_to(whole, (4,) + whole.shape), "y")
    whole = whole.reshape(4, 2, layers, rank, count // 4, positions)
    whole = whole.transpose(1, 2, 3, 0, 4, 5).reshape(2, layers, rank, count, positions)
    grad_down = jnp.einsum("lres,lesd->lred", whole[0], acts, preferred_element_type=F32)
    grad_up = jnp.einsum("lres,lesd->lred", whole[1], cotangents, preferred_element_type=F32)
    grads = jnp.stack([grad_down, grad_up]).astype(BF16).reshape(8, rows // 8, count, width)
    own = swap(grads, ("x", "zh"))
    other = lax.ppermute(own, "c", [(0, 1), (1, 0)])
    own = own.transpose(0, 2, 1, 3).reshape(8, count, -1)
    other = other.transpose(0, 2, 1, 3).reshape(8, count, -1)
    both = jnp.stack([own, other], 1)
    gram = jnp.einsum("aek,bsfk->aebsf", own, both, preferred_element_type=F32)
    sq = jnp.sum(jnp.square(both.astype(F32)), -1)
    side = 2 * count
    gram = gram.reshape(4, side, 4, 2 * side).transpose(0, 2, 1, 3)
    row_sq = jnp.broadcast_to(sq.reshape(1, 4, 1, 2 * side), (4, 4, 1, 2 * side))
    col_sq = jnp.broadcast_to(sq[:, 0].reshape(4, 1, 1, side), (4, 4, 1, side))
    col_sq = jnp.pad(col_sq, ((0, 0), (0, 0), (0, 0), (0, side)))
    sent = jnp.concatenate([gram, row_sq, col_sq], 2).reshape(16, side + 2, 2 * side)
    got = jnp.sum(swap(sent, ("x", "y")), 0)
    ordered = got.reshape(side + 2, 2, 2, count)
    ordered = jnp.where(lax.axis_index("c") == 0, ordered, ordered[:, :, ::-1])
    half = count // 2
    tiles = ordered[:side].reshape(2, count, 8, half).transpose(0, 2, 1, 3).reshape(16, count * half)
    row_sq = jnp.broadcast_to(ordered[side].reshape(1, 8, half), (2, 8, half)).reshape(16, half)
    col_sq = jnp.broadcast_to(got[side + 1, :side].reshape(2, 1, count), (2, 8, count)).reshape(16, count)
    sent = jnp.concatenate([tiles, row_sq, col_sq], 1)
    sent = jnp.pad(sent, ((0, 0), (0, 128 - half - count))).reshape(16, -1, 128)
    got = jnp.sum(swap(sent, ("zh", "zl")), 0).reshape(-1)
    size = count * half
    tile = got[:size].reshape(count, half).T
    row_sq = got[size : size + half]
    col_sq = got[size + half : size + half + count]
    return tile * lax.rsqrt(row_sq + 1e-06)[:, None] * lax.rsqrt(col_sq + 1e-06)[None, :]


def solution(mesh):
    fine = Mesh(mesh.devices.reshape(4, 2, 2, 4, 8), ("x", "zh", "c", "y", "zl"))
    grp, hid = ("x", "zh", "c"), ("y", "zl")
    return jax.shard_map(
        local,
        mesh=fine,
        in_specs=(
            P(None, grp, None, hid),
            P(None, grp, None, hid),
            P(None, None, hid),
            P(None, hid, None),
            P(grp),
        ),
        out_specs=P(hid, grp),
        check_vma=False,
    )
```

time: 918 us -> 153 us (0.17)
  waiting for transfers between devices: 429 us -> 11.1 us
  blocking collectives: 429 us -> 116 us
  starting transfers between devices: 28.8 us -> 7.74 us
  between operations: 14.1 us -> 0.26 us
    psum x2 -> x0, blocking collectives: 372 us -> none  [the longest x1 256 us: local(): up_sum, down_sum = lax.psum((up_factor, down_factor), 'hid')]
    ppermute x15 -> x1, waiting for transfers between devices: 370 us -> 0.49 us  [local(): other = lax.ppermute(own, 'c', [(0, 1), (1, 0)])]
    all_to_all x0 -> x6, blocking collectives: none -> 116 us  [swap(): return lax.all_to_all(block, axes, 0, 0, tiled=True)]
    reduce_scatter x1 -> x0, waiting for transfers between devices: 58.7 us -> none  [local(): share = lax.psum_scatter(accum, 'hid', scatter_dimension=0, tiled=True)]
    unnamed x1 -> x0, blocking collectives: 57.2 us -> none
    ppermute x15 -> x1, starting transfers between devices: 28.8 us -> 1.91 us  [local(): other = lax.ppermute(own, 'c', [(0, 1), (1, 0)])]
    all_to_all x0 -> x1, waiting for transfers between devices: none -> 10.6 us  [swap(): return lax.all_to_all(block, axes, 0, 0, tiled=True)]
  transfers between devices with their start and end apart: 16 -> 2, of which waited for: 16 -> 2; matrix products, arithmetic and copies ran while one was open for 1% -> 1% of each run, Pallas kernels for 0% -> 0%
where the time goes in v1:
time: 153 us; the launch traced here: 151 us
  blocking collectives  116 us (76%)
  waiting for transfers between devices  11.1 us (7%)
  local copies, waits for them, and re-layouts  8.68 us (6%)
  starting transfers between devices  7.74 us (5%)
  matrix products  4.82 us (3%)
  other arithmetic  2.83 us (2%)
    all_to_all x6, blocking collectives, swap(): return lax.all_to_all(block, axes, 0, 0, tiled=True)  116 us
    all_to_all x1, waiting for transfers between devices, swap(): return lax.all_to_all(block, axes, 0, 0, tiled=True)  10.6 us
    all_to_all x1, starting transfers between devices, swap(): return lax.all_to_all(block, axes, 0, 0, tiled=True)  5.83 us
  transfers between devices with their start and end apart: 2, of which 2 were waited for; matrix products, arithmetic and copies ran while one was open for 1% of the time, Pallas kernels for 0%

profile of v1, /device:TPU:6, one launch (start us, length us, event | category | flops | bytes accessed | tf_op | source)
XLA Modules:
  0.0 151.3 jit_solution(5537354226500278740)
XLA Ops:
  0.0 1.2 copy-done
  1.2 1.6 %convolution_bitcast_fusion.1 = f32[1,2,16,32,64]{4,2,3,1,0:T(8,128)S(1)} fusion(bf16[2,32,64,128]{3,2,1,0:T(8,128)(2,1)S(1)} %copy-done, bf16[2,16,128]{2,1,0:T(8,128)(2,1)} %param.7), kind=kOutput, calls=%fused_computation.2 | convolution fusion | flops 16777216 | bytes 1318912 | tf_op jit(solution)/shard_map/lesd,lrd->lres/dot_general | solution.py:18
  2.8 0.9 convolution_bitcast_fusion.2
  3.9 0.3 copy.39
  4.2 1.1 stack.29
  5.7 1.2 select_bitcast_fusion
  6.9 0.2 copy.40
  7.1 13.7 %all_to_all.35 = f32[4,64,512]{2,1,0:T(8,128)S(1)} all-to-all(f32[4,64,512]{2,1,0:T(8,128)S(1)} %copy.40), channel_id=1, replica_groups=mesh['x'=4,'zh'=2,'c'=2,'y'=4,'zl'=8] {'y'}, dimensions={0} | all-to-all | bytes 1048576 | tf_op jit(solution)/shard_map/all_to_all | solution.py:11
  20.8 23.8 %all_to_all.36 = f32[8,8,512]{2,1,0:T(8,128)S(1)} all-to-all(f32[8,8,512]{2,1,0:T(8,128)S(1)} %bitcast.82), channel_id=1, replica_groups=mesh['x'=4,'zh'=2,'c'=2,'y'=4,'zl'=8] {'zl'}, dimensions={0} | all-to-all | bytes 262144 | tf_op jit(solution)/shard_map/all_to_all | solution.py:11
  44.6 14.3 %all_to_all.37 = bf16[8,8,512]{2,1,0:T(8,128)(2,1)S(1)} all-to-all(bf16[8,8,512]{2,1,0:T(8,128)(2,1)S(1)} %broadcast_in_dim.47), channel_id=1, replica_groups=mesh['x'=4,'zh'=2,'c'=2,'y'=4,'zl'=8] {'zl'}, dimensions={0} | all-to-all | bytes 131072 | tf_op jit(solution)/shard_map/all_to_all | solution.py:11
  59.0 9.1 %all_to_all.38 = bf16[4,64,512]{2,1,0:T(8,128)(2,1)S(1)} all-to-all(bf16[4,64,512]{2,1,0:T(8,128)(2,1)S(1)} %broadcast_in_dim.48), channel_id=1, replica_groups=mesh['x'=4,'zh'=2,'c'=2,'y'=4,'zl'=8] {'y'}, dimensions={0} | all-to-all | bytes 524288 | tf_op jit(solution)/shard_map/all_to_all | solution.py:11
  68.0 0.3 reshape.71
  68.4 0.4 fusion
  68.8 0.4 fusion.1
  69.4 31.5 %all_to_all.39 = bf16[8,8,32,128]{3,2,1,0:T(8,128)(2,1)S(1)} all-to-all(bf16[8,8,32,128]{3,2,1,0:T(8,128)(2,1)S(1)} %bitcast.77), channel_id=1, replica_groups=mesh['x'=4,'zh'=2,'c'=2,'y'=4,'zl'=8] {'x','zh'}, dimensions={0} | all-to-all | bytes 1048576 | tf_op jit(solution)/shard_map/all_to_all | solution.py:11
  100.9 1.9 %collective-permute-start = (bf16[8,8,32,128]{3,2,1,0:T(8,128)(2,1)S(1)}, bf16[8,8,32,128]{3,2,1,0:T(8,128)(2,1)}, u32[]{:S(2)}, u32[]{:S(2)}) collective-permute-start(bf16[8,8,32,128]{3,2,1,0:T(8,128)(2,1)S(1)} %all_to_all.39), channel_id=1, source_target_pairs={{0,32},{32,0},{1,33},{33,1},{2,34},{34,2},{3,35},{35,3},{4,36},{36... | collective-permute-start | bytes 1572872 | tf_op jit(solution)/shard_map/ppermute | solution.py:34
  102.8 0.2 copy.44
  103.0 0.2 stack_reshape.6
  103.3 1.0 reshape.83
  104.3 0.5 collective-permute-done
  104.8 1.3 copy.46
  106.1 0.2 stack_reshape.7
  106.4 0.3 multiply_reduce_fusion
  106.9 1.5 convolution_bitcast_fusion
  108.5 0.9 select_maximum_fusion
  109.3 5.8 %all-to-all-start.5 = ((f32[16,66,128]{2,1,0:T(8,128)}), f32[16,66,128]{2,1,0:T(8,128)S(1)}, u32[]{:S(2)}, u32[]{:S(2)}) async-start(f32[16,66,128]{2,1,0:T(8,128)} %bitcast.23), calls=%async_computation.5 | async-start | bytes 1179648 | tf_op jit(solution)/shard_map/all_to_all | solution.py:11
  115.1 10.6 %all-to-all-done.5 = f32[16,66,128]{2,1,0:T(8,128)S(1)} async-done(((f32[16,66,128]{2,1,0:T(8,128)}), f32[16,66,128]{2,1,0:T(8,128)S(1)}, u32[]{:S(2)}, u32[]{:S(2)}) %all-to-all-start.5) | async-done | bytes 540704 | tf_op jit(solution)/shard_map/all_to_all | solution.py:11
  125.9 0.2 slice_reduce_fusion
  126.3 0.1 copy.50
  126.4 0.2 reshape.75
  126.8 23.5 %all_to_all.40 = f32[16,5,128]{2,1,0:T(8,128)S(1)} all-to-all(f32[16,5,128]{2,1,0:T(8,128)S(1)} %reshape.78), channel_id=1, replica_groups=mesh['x'=4,'zh'=2,'c'=2,'y'=4,'zl'=8] {'zh','zl'}, dimensions={0} | all-to-all | bytes 81920 | tf_op jit(solution)/shard_map/all_to_all | solution.py:11
  150.6 0.7 copy.51
  (49 shorter events, 2.0 us)
Async XLA Ops:
  0.0 1.2 copy-start
  0.0 2.8 %copy-start.1 = (bf16[2,32,64,128]{3,2,1,0:T(8,128)(2,1)S(1)}, bf16[2,32,64,128]{3,2,1,0:T(8,128)(2,1)}, u32[]{:S(2)}) copy-start(bf16[2,32,64,128]{3,2,1,0:T(8,128)(2,1)} %param.6) | copy-start | bytes 3145732
  0.0 2.8 %copy-start.2 = (bf16[2,128,16]{1,2,0:T(8,128)(2,1)S(1)}, bf16[2,128,16]{1,2,0:T(8,128)(2,1)}, u32[]{:S(2)}) copy-start(bf16[2,128,16]{1,2,0:T(8,128)(2,1)} %param.8) | copy-start | bytes 24580
  4.2 1.2 copy-start.3
  100.9 3.9 %collective-permute-start = (bf16[8,8,32,128]{3,2,1,0:T(8,128)(2,1)S(1)}, bf16[8,8,32,128]{3,2,1,0:T(8,128)(2,1)}, u32[]{:S(2)}, u32[]{:S(2)}) collective-permute-start(bf16[8,8,32,128]{3,2,1,0:T(8,128)(2,1)S(1)} %all_to_all.39), channel_id=1, source_target_pairs={{0,32},{32,0},{1,33},{33,1},{2,34},{34,2},{3,35},{35,3},{4,36},{36... | collective-permute-start | bytes 1572872 | tf_op jit(solution)/shard_map/ppermute | solution.py:34
  109.3 16.5 %all-to-all-start.5 = ((f32[16,66,128]{2,1,0:T(8,128)}), f32[16,66,128]{2,1,0:T(8,128)S(1)}, u32[]{:S(2)}, u32[]{:S(2)}) async-start(f32[16,66,128]{2,1,0:T(8,128)} %bitcast.23), calls=%async_computation.5 | async-start | bytes 1179648 | tf_op jit(solution)/shard_map/all_to_all | solution.py:11
